TPU v7x, 32 devices: a whole 2x2x4 slice. The times are simulated.
32 devices in a mesh: cand: 2 (over y), gx: 4 (over z), gy: 2 (over x), wa: 2 (over core).
Axes of the slice: x: 2, y: 2, z: 4, core: 2. Of those that a mesh axis runs over, the one named last changes fastest.
Arguments:
- field: bfloat16 [4, 4, 2, 4, 4, 128, 128], P('wa', 'cand', None, 'gx', None, 'gy'), parts along dimension 1, may hold values from -6 to 6
- active_rows: int32 [4, 4], P('gx'), may hold values from 0 to 128, as said below
- kern: bfloat16 [4, 2, 4, 64, 128], P('wa'), may hold values from -0.25 to 0.25
- target: float32 [4, 64, 64], P('wa'), may hold values from 0 to 3
Outputs:
- design_grad: float32 [4, 8, 128, 128], P('gx', 'cand', 'gy'), parts along dimension 1
- intensity: float32 [4, 128, 64], P('wa', 'cand'), parts along dimension 1
There are 2 independent parts, one for each index of `cand`. A program takes and returns all parts, laid end to end along the dimension named above; an argument that names none is the same for every part. Nothing has to cross between parts.
Inputs may be any that keep to these rules, and one draw needn't show every extreme that they name: `active_rows`: live rows are counted from a tile's first cell row; tiles near the aperture's centre are full and its corners empty.
All inputs are finite; a program needn't handle non-finite values.
Results may differ from a plain program's by a relative error of at most 0.0075.
Values may be sent and summed in bfloat16 or wider, within the bound.
A program may use at most 128 MiB of HBM per device.

v0:
```python
import jax
import jax.numpy as jnp
from jax import lax
from jax.sharding import PartitionSpec as P

FP = 64


def product(form, first, second):
    return jnp.einsum(form, first, second, preferred_element_type=jnp.float32)


def precise(form, first, second):
    return jnp.einsum(
        form, first, second, precision=lax.Precision.HIGHEST, preferred_element_type=jnp.float32
    )


def on_device(field, active_rows, kern, target):
    tile_row = lax.axis_index("gx")
    block = lax.axis_index("gy")
    tiles = field.shape[4]
    rows_dev = field.shape[5]
    side = field.shape[6]
    first_row = block * rows_dev
    local_rows = first_row + jnp.arange(rows_dev, dtype=jnp.int32)
    live = local_rows[None, :, None] < active_rows[0][:, None, None]
    masked = jnp.where(live, field[:, :, :, 0], jnp.zeros((), field.dtype))
    plane_real = masked[:, :, 0]
    plane_imag = masked[:, :, 1]
    kern_real = kern[:, 0]
    kern_imag = kern[:, 1]
    inner_real = product("lsjuv,ljqv->lsuq", plane_real, kern_real) - product(
        "lsjuv,ljqv->lsuq", plane_imag, kern_imag
    )
    inner_imag = product("lsjuv,ljqv->lsuq", plane_real, kern_imag) + product(
        "lsjuv,ljqv->lsuq", plane_imag, kern_real
    )
    own_kern = lax.dynamic_index_in_dim(kern, tile_row, axis=2, keepdims=False)
    own_kern = lax.dynamic_slice_in_dim(own_kern, first_row, rows_dev, axis=3)
    own_real = own_kern[:, 0].astype(jnp.float32)
    own_imag = own_kern[:, 1].astype(jnp.float32)
    focal_real = precise("lpu,lsuq->lspq", own_real, inner_real) - precise(
        "lpu,lsuq->lspq", own_imag, inner_imag
    )
    focal_imag = precise("lpu,lsuq->lspq", own_real, inner_imag) + precise(
        "lpu,lsuq->lspq", own_imag, inner_real
    )
    focal_real, focal_imag = lax.psum((focal_real, focal_imag), ("gx", "gy"))
    intensity = jnp.sum(focal_real * focal_real + focal_imag * focal_imag, axis=1)
    excess = (intensity - target)[:, None]
    source_real = excess * focal_real
    source_imag = excess * focal_imag
    scale = jnp.float32(tiles * side / FP)
    row_real = (
        precise("lpu,lspq->lsuq", own_real, source_real)
        + precise("lpu,lspq->lsuq", own_imag, source_imag)
    ).astype(jnp.bfloat16)
    row_imag = (
        precise("lpu,lspq->lsuq", own_real, source_imag)
        - precise("lpu,lspq->lsuq", own_imag, source_real)
    ).astype(jnp.bfloat16)
    back_real = product("lsuq,ljqv->lsjuv", row_real, kern_real) + product(
        "lsuq,ljqv->lsjuv", row_imag, kern_imag
    )
    back_imag = product("lsuq,ljqv->lsjuv", row_imag, kern_real) - product(
        "lsuq,ljqv->lsjuv", row_real, kern_imag
    )
    own_terms = back_real * plane_real.astype(jnp.float32) + back_imag * plane_imag.astype(
        jnp.float32
    )
    partial_value = scale * jnp.sum(own_terms, axis=(0, 1))
    summed = lax.psum(partial_value.astype(jnp.bfloat16), "wa").astype(jnp.float32)
    partner = lax.all_to_all(
        lax.all_to_all(summed.astype(jnp.bfloat16), "gx", split_axis=0, concat_axis=0, tiled=True),
        "gy",
        split_axis=2,
        concat_axis=1,
        tiled=True,
    ).astype(summed.dtype)
    design_grad = 0.5 * (summed + jnp.swapaxes(partner, 1, 2))
    return (design_grad[None], intensity)


def solution(mesh):
    placed = (
        P("wa", "cand", None, "gx", None, "gy", None),
        P("gx", None),
        P("wa", None, None, None, None),
        P("wa", None, None),
    )
    return jax.shard_map(
        on_device,
        mesh=mesh,
        in_specs=placed,
        out_specs=(P("gx", "cand", "gy", None), P("wa", "cand", None)),
        check_vma=False,
    )
```

profile of v0, /device:TPU:0, one launch (start us, length us, event | category | flops | bytes accessed | tf_op | source)
XLA Modules:
  0.0 136.3 jit_solution(17676847374566046636)
XLA Ops:
  7.2 0.0 all-reduce.6.cloned.1.call-start
  7.2 0.0 copy-start.5
  7.2 0.6 copy-done.5
  7.9 0.1 broadcast_compare_fusion
  8.0 0.0 copy-start
  8.0 1.2 bitcast_select_fusion
  9.2 0.0 copy-done
  9.2 0.2 convolution_bitcast_fusion
  9.4 0.2 convolution_bitcast_fusion.2
  9.6 0.2 fusion.9
  9.8 0.2 fusion.8
  10.0 0.1 copy_bitcast_fusion.1
  10.1 0.3 fusion.44
  10.4 0.3 fusion.45
  10.7 0.9 fusion.6
  11.7 0.9 fusion.7
  12.6 0.0 copy-start.4
  12.6 0.0 all-reduce.6.cloned.1.call-update
  12.6 0.0 all-reduce.4.cloned.1.call-start
  12.7 0.8 copy-done.4
  13.4 0.1 copy.44
  13.5 72.8 %all-reduce.6.cloned.1.call-done = (f32[2,2,64,64]{2,3,1,0:T(8,128)}, f32[2,2,64,64]{2,3,1,0:T(8,128)}) async-done(((f32[2,2,64,64]{2,3,1,0:T(8,128)}, f32[2,2,64,64]{2,3,1,0:T(8,128)}), (f32[2,2,64,64]{2,3,1,0:T(8,128)}, f32[2,2,64,64]{2,3,1,0:T(8,128)})) %all-reduce.6.cloned.1.call-update) | async-done | bytes 131088 | tf_op jit(solution)/shard_map/psum | solution.py:49
  86.3 1.0 add_reduce_fusion
  87.3 0.0 copy-start.1
  87.4 0.9 copy-done.1
  88.2 0.0 copy-start.2
  88.2 0.2 fusion.26
  88.4 0.7 copy-done.2
  89.1 0.2 fusion.30
  89.3 0.2 fusion.12
  89.5 0.2 fusion.13
  89.8 0.3 fusion.20
  90.0 0.3 fusion.18
  90.3 0.3 fusion.4
  90.6 0.3 fusion.5
  90.9 0.6 multiply_convert_fusion
  91.5 0.0 all-reduce.4.cloned.1.call-update
  91.5 17.2 %all-reduce.4.cloned.1.call-done = bf16[4,64,128]{2,1,0:T(8,128)(2,1)} async-done(((bf16[4,64,128]{2,1,0:T(8,128)(2,1)}), bf16[4,64,128]{2,1,0:T(8,128)(2,1)}) %all-reduce.4.cloned.1.call-update) | async-done | bytes 65552 | tf_op jit(solution)/shard_map/psum | solution.py:73
  108.7 10.6 %all_to_all.14 = bf16[4,64,128]{2,1,0:T(8,128)(2,1)S(1)} all-to-all(bf16[4,64,128]{2,1,0:T(8,128)(2,1)} %all-reduce.4.cloned.1.call-done), channel_id=1, replica_groups=mesh['cand'=2,'gx'=4,'gy'=2,'wa'=2] {'gx'}, dimensions={0} | all-to-all | bytes 131072 | tf_op jit(solution)/shard_map/all_to_all | solution.py:75
  119.3 0.1 copy.49
  119.4 0.8 reshape.52
  120.2 3.3 %all-to-all-start.1 = ((bf16[2,2,8192]{2,1,0:T(2,128)(2,1)}), bf16[2,2,8192]{2,1,0:T(2,128)(2,1)S(1)}, u32[]{:S(2)}, u32[]{:S(2)}) async-start(bf16[2,2,8192]{2,1,0:T(2,128)(2,1)} %reshape.52), calls=%async_computation.1 | async-start | bytes 131072 | tf_op jit(solution)/shard_map/all_to_all | solution.py:74
  123.5 0.7 copy.51
  124.3 3.4 %all-to-all-done.1 = bf16[2,2,8192]{2,1,0:T(2,128)(2,1)S(1)} async-done(((bf16[2,2,8192]{2,1,0:T(2,128)(2,1)}), bf16[2,2,8192]{2,1,0:T(2,128)(2,1)S(1)}, u32[]{:S(2)}, u32[]{:S(2)}) %all-to-all-start.1) | async-done | bytes 65568 | tf_op jit(solution)/shard_map/all_to_all | solution.py:74
  127.7 0.1 reshape.53
  127.8 0.1 copy.81
  127.9 0.0 copy-start.3
  128.0 0.2 reshape.38
  128.1 0.6 copy-done.3
  128.8 0.7 fusion.25
  (2 shorter events, 0.0 us)
Async XLA Ops:
  7.2 79.2 %all-reduce.6.cloned.1.call-start = ((), (), s32[]{:S(2)}) async-start(), calls=%async_computation.3 | async-start | bytes 524288 | tf_op jit(solution)/shard_map/psum | solution.py:49
  7.2 0.7 copy-start.5
  8.0 1.2 copy-start
  12.6 0.8 copy-start.4
  12.6 96.1 %all-reduce.4.cloned.1.call-start = ((), (), s32[]{:S(2)}) async-start(), calls=%async_computation.2 | async-start | bytes 131072 | tf_op jit(solution)/shard_map/psum | solution.py:73
  87.3 0.9 copy-start.1
  88.2 0.9 copy-start.2
  120.2 7.4 %all-to-all-start.1 = ((bf16[2,2,8192]{2,1,0:T(2,128)(2,1)}), bf16[2,2,8192]{2,1,0:T(2,128)(2,1)S(1)}, u32[]{:S(2)}, u32[]{:S(2)}) async-start(bf16[2,2,8192]{2,1,0:T(2,128)(2,1)} %reshape.52), calls=%async_computation.1 | async-start | bytes 131072 | tf_op jit(solution)/shard_map/all_to_all | solution.py:74
  127.9 0.8 copy-start.3
Sparse Core Ops, SparseCore 0:
  12.8 73.5 all-reduce.5
  91.7 16.9 all-reduce.3
where the time goes:
time: 137 us; the launch traced here: 136 us
  waiting for transfers between devices  93.4 us (68%)
  between operations  14.3 us (10%)
  blocking collectives  10.6 us (8%)
  local copies, waits for them, and re-layouts  5.93 us (4%)
  matrix products  5.16 us (4%)
  other arithmetic  3.59 us (3%)
  starting transfers between devices  3.38 us (2%)
    psum x1, waiting for transfers between devices, on_device(): focal_real, focal_imag = lax.psum((focal_real, focal_imag), ('gx', 'gy'))  72.8 us
    psum x1, waiting for transfers between devices, on_device(): lax.psum(partial_value.astype(jnp.bfloat16), 'wa').astype(jnp.float32)  17.2 us
    all_to_all x1, blocking collectives, on_device(): lax.all_to_all(summed.astype(jnp.bfloat16), 'gx', split_axis=0, concat_ax...  10.6 us
    unnamed x16, local copies, waits for them, and re-layouts  5.38 us
    all_to_all x1, waiting for transfers between devices, on_device(): lax.all_to_all(lax.all_to_all(summed.astype(jnp.bfloat16), 'gx', split_ax...  3.39 us
    all_to_all x1, starting transfers between devices, on_device(): lax.all_to_all(lax.all_to_all(summed.astype(jnp.bfloat16), 'gx', split_ax...  3.3 us
    dot_general x8, matrix products, precise(): jnp.einsum(form, first, second, precision=lax.Precision.HIGHEST, preferre...  3.24 us
  transfers between devices with their start and end apart: 3, of which 3 were waited for; matrix products, arithmetic and copies ran while one was open for 1% of the time, Pallas kernels for 0%

commit v1 on v0

v1 whole, which is shorter than its diff:
```python
import functools

import jax
import jax.numpy as jnp
from jax import lax
from jax.experimental import pallas as pl
from jax.experimental.pallas import tpu as pltpu
from jax.sharding import PartitionSpec as P

MESH = pl.DeviceIdType.MESH
SHARD_ROWS = 16
LANES = 128


def each(count, body):
    if count <= 16:
        for step in range(count):
            body(step)
    else:
        lax.fori_loop(0, count, lambda step, carry: (body(step), carry)[1], 0)


def times_i(value):
    parts = []
    for first in range(0, value.shape[1], LANES):
        part = pltpu.roll(value[:, first : first + LANES], LANES // 2, 1)
        lane = lax.broadcasted_iota(jnp.int32, part.shape, 1)
        parts.append(jnp.where(lane < LANES // 2, -part, part))
    return jnp.concatenate(parts, axis=1)


def kernel(
    nx, ny, field, rows, kern, target, grad, inten,
    plane, weights, fpart, frecv, src, ibuf, pown, ppeer, total, tsend, trecv,
    rs_send, rs_recv, ag_send, ag_recv, in_send, in_recv, wa_send, wa_recv, tr_send, tr_recv,
):
    n = nx * ny
    gx, gy, wa = lax.axis_index("gx"), lax.axis_index("gy"), lax.axis_index("wa")
    me = gx * ny + gy
    waves, pols, _, _, tiles, side_u, side = field.shape
    fp = kern.shape[3]
    per_wave = fp // SHARD_ROWS
    owners = waves * per_wave
    group = side // side_u

    def peer_of(step):
        return lax.rem(me + step + 1, n)

    def place(peer):
        return {"gx": peer // ny, "gy": lax.rem(peer, ny)}

    barrier = pltpu.get_barrier_semaphore()

    def greet(step):
        pl.semaphore_signal(barrier, inc=1, device_id=place(peer_of(step)), device_id_type=MESH)

    each(n - 1, greet)
    pl.semaphore_signal(barrier, inc=1, device_id={"wa": 1 - wa}, device_id_type=MESH)

    def shard_copy(owner, slot):
        return pltpu.make_async_remote_copy(
            src_ref=fpart.at[owner], dst_ref=frecv.at[slot],
            send_sem=rs_send.at[owner], recv_sem=rs_recv.at[slot],
            device_id=place(owner), device_id_type=MESH,
        )

    row_index = lax.broadcasted_iota(jnp.int32, (side_u, side), 0) + gy * side_u
    for l in range(waves):
        for j in range(tiles):
            real, imag = kern[l, 0, j], kern[l, 1, j]
            at = 2 * side * j
            weights[l, :fp, at : at + side] = real
            weights[l, :fp, at + side : at + 2 * side] = -imag
            weights[l, fp:, at : at + side] = imag
            weights[l, fp:, at + side : at + 2 * side] = real
            live = row_index < rows[0, j]
            for s in range(pols):
                for c in range(2):
                    value = field[l, s, c, 0, j].astype(jnp.float32)
                    plane[l, s * side_u : (s + 1) * side_u, at + c * side : at + (c + 1) * side] = jnp.where(
                        live, value, 0.0
                    ).astype(jnp.bfloat16)
        inner = lax.dot_general(
            plane[l], weights[l], (((1,), (1,)), ((), ())), preferred_element_type=jnp.float32
        )
        inner = jnp.concatenate(
            [inner[s * side_u : (s + 1) * side_u] for s in range(pols)], axis=1
        )
        both = []
        for value in (inner, times_i(inner)):
            both += [jnp.where(gy == k, value, 0.0) for k in range(group)]
        both = jnp.concatenate(both, axis=0)
        high = both.astype(jnp.bfloat16)
        low = (both - high.astype(jnp.float32)).astype(jnp.bfloat16)
        own = jnp.concatenate([kern[l, 0, gx], kern[l, 1, gx]], axis=1)
        focal = jnp.dot(own, high, preferred_element_type=jnp.float32) + jnp.dot(
            own, low, preferred_element_type=jnp.float32
        )
        for k in range(per_wave):
            fpart[l * per_wave + k] = focal[k * SHARD_ROWS : (k + 1) * SHARD_ROWS]
        if l == 0:
            pl.semaphore_wait(barrier, n)
        for k in range(per_wave):
            owner = l * per_wave + lax.rem(me + k, per_wave)

            @pl.when(owner != me)
            def _():
                shard_copy(owner, me).start()

    def source_copy(peer, slot):
        return pltpu.make_async_remote_copy(
            src_ref=src.at[slot], dst_ref=src.at[slot],
            send_sem=ag_send.at[peer], recv_sem=ag_recv.at[slot],
            device_id=place(peer), device_id_type=MESH,
        )

    def intensity_copy(peer, slot):
        return pltpu.make_async_remote_copy(
            src_ref=ibuf.at[slot], dst_ref=ibuf.at[slot],
            send_sem=in_send.at[peer], recv_sem=in_recv.at[slot],
            device_id=place(peer), device_id_type=MESH,
        )

    def owned():
        frecv[me] = fpart[me]

        def arrive(step):
            shard_copy(me, peer_of(step)).wait_recv()

        each(n - 1, arrive)
        if n <= 16:
            focal = frecv[0]
            for slot in range(1, n):
                focal = focal + frecv[slot]
        else:
            focal = lax.fori_loop(
                1, n, lambda slot, value: value + frecv[slot], frecv[0]
            )
        square = focal * focal
        bright = square[:, :LANES]
        for s in range(1, pols):
            bright = bright + square[:, s * LANES : (s + 1) * LANES]
        bright = bright + pltpu.roll(bright, LANES // 2, 1)
        first = pl.multiple_of(lax.rem(me, per_wave) * SHARD_ROWS, SHARD_ROWS)
        goal = target[me // per_wave, pl.ds(first, SHARD_ROWS), :]
        excess = bright - jnp.concatenate([goal, goal], axis=1)
        src[me] = (focal * jnp.concatenate([excess] * pols, axis=1)).astype(jnp.bfloat16)
        each(n - 1, lambda step: source_copy(peer_of(step), me).start())
        half = SHARD_ROWS // 2
        lane = lax.broadcasted_iota(jnp.int32, (half, LANES), 1)
        ibuf[me] = jnp.where(lane < LANES // 2, bright[:half], bright[half:])
        each(n - 1, lambda step: intensity_copy(peer_of(step), me).start())

    if n > owners:
        pl.when(me < owners)(owned)
    else:
        owned()

    for l in range(waves):
        for k in range(per_wave):
            owner = l * per_wave + k

            @pl.when(owner != me)
            def _():
                source_copy(owner, owner).wait_recv()

        source = src[l * per_wave : (l + 1) * per_wave].reshape(fp, pols * LANES)
        turned = (-times_i(source.astype(jnp.float32))).astype(jnp.bfloat16)
        own = kern[l, :, gx].reshape(2 * fp, side)
        side_rows = lax.dot_general(
            own, jnp.concatenate([source, turned], axis=0), (((0,), (0,)), ((), ())),
            preferred_element_type=jnp.float32,
        )
        picked = side_rows[:side_u]
        for k in range(1, group):
            picked = jnp.where(gy == k, side_rows[k * side_u : (k + 1) * side_u], picked)
        picked = jnp.concatenate(
            [picked[:, s * LANES : (s + 1) * LANES] for s in range(pols)], axis=0
        ).astype(jnp.bfloat16)
        for j in range(tiles):
            at = 2 * side * j
            back = jnp.dot(
                picked, weights[l, :, at : at + 2 * side], preferred_element_type=jnp.float32
            )
            terms = back * plane[l, :, at : at + 2 * side].astype(jnp.float32)
            terms = terms[:, :side] + terms[:, side:]
            value = terms[:side_u]
            for s in range(1, pols):
                value = value + terms[s * side_u : (s + 1) * side_u]
            if l > 0:
                value = value + total[j]
            if l < waves - 1:
                total[j] = value
            else:
                pown[j] = (value * jnp.float32(tiles * side / fp)).astype(jnp.bfloat16)

    swap = pltpu.make_async_remote_copy(
        src_ref=pown, dst_ref=ppeer, send_sem=wa_send, recv_sem=wa_recv,
        device_id={"wa": 1 - wa}, device_id_type=MESH,
    )
    swap.start()

    for owner in range(owners):
        @pl.when(owner != me)
        def _():
            intensity_copy(owner, owner).wait_recv()

        l, first, half = owner // per_wave, owner % per_wave * SHARD_ROWS, SHARD_ROWS // 2
        value = ibuf[owner]
        inten[l, first : first + half, :] = value[:, : LANES // 2]
        inten[l, first + half : first + 2 * half, :] = value[:, LANES // 2 :]

    swap.wait()

    packs = tsend.shape[2] // side_u
    short = side_u // packs
    for j in range(tiles):
        value = pown[j].astype(jnp.float32) + ppeer[j].astype(jnp.float32)
        total[j] = value
        turned = value.T
        for k in range(ny):
            block = turned[k * side_u : (k + 1) * side_u]
            block = jnp.concatenate(
                [block[g * short : (g + 1) * short] for g in range(packs)], axis=1
            )
            tsend[j * ny + k] = block.astype(jnp.bfloat16)

    def turned_copy(peer, slot):
        return pltpu.make_async_remote_copy(
            src_ref=tsend.at[peer], dst_ref=trecv.at[slot],
            send_sem=tr_send.at[peer], recv_sem=tr_recv.at[slot],
            device_id=place(peer), device_id_type=MESH,
        )

    each(n - 1, lambda step: turned_copy(peer_of(step), me).start())
    trecv[me] = tsend[me]
    each(n - 1, lambda step: turned_copy(me, peer_of(step)).wait_recv())
    for j in range(tiles):
        blocks = [trecv[j * ny + k].astype(jnp.float32) for k in range(ny)]
        lines = [
            jnp.concatenate([block[:, g * side_u : (g + 1) * side_u] for block in blocks], axis=1)
            for g in range(packs)
        ]
        grad[0, j] = 0.5 * (total[j] + jnp.concatenate(lines, axis=0))

    for owner in range(owners):
        @pl.when(owner != me)
        def _():
            shard_copy(owner, me).wait_send()

    def drain_owned():
        each(n - 1, lambda step: source_copy(peer_of(step), me).wait_send())
        each(n - 1, lambda step: intensity_copy(peer_of(step), me).wait_send())

    if n > owners:
        pl.when(me < owners)(drain_owned)
    else:
        drain_owned()
    each(n - 1, lambda step: turned_copy(peer_of(step), me).wait_send())


def on_device(nx, ny, field, active_rows, kern, target):
    waves, pols, _, _, tiles, side_u, side = field.shape
    fp = kern.shape[3]
    n = nx * ny
    owners = waves * (fp // SHARD_ROWS)
    packs = LANES // side_u
    if (side_u // packs) % 16:
        packs = 1
    turned = (n, side_u // packs, side_u * packs)
    dma = pltpu.SemaphoreType.DMA
    vmem = pl.BlockSpec(memory_space=pltpu.VMEM)
    width = pols * LANES
    return pl.pallas_call(
        functools.partial(kernel, nx, ny),
        out_shape=(
            jax.ShapeDtypeStruct((1, tiles, side_u, side), jnp.float32),
            jax.ShapeDtypeStruct((waves, fp, fp), jnp.float32),
        ),
        in_specs=[vmem, pl.BlockSpec(memory_space=pltpu.SMEM), vmem, vmem],
        out_specs=(vmem, vmem),
        scratch_shapes=[
            pltpu.VMEM((waves, pols * side_u, tiles * 2 * side), jnp.bfloat16),
            pltpu.VMEM((waves, 2 * fp, tiles * 2 * side), jnp.bfloat16),
            pltpu.VMEM((owners, SHARD_ROWS, width), jnp.float32),
            pltpu.VMEM((n, SHARD_ROWS, width), jnp.float32),
            pltpu.VMEM((owners, SHARD_ROWS, width), jnp.bfloat16),
            pltpu.VMEM((owners, SHARD_ROWS // 2, LANES), jnp.float32),
            pltpu.VMEM((tiles, side_u, side), jnp.bfloat16),
            pltpu.VMEM((tiles, side_u, side), jnp.bfloat16),
            pltpu.VMEM((tiles, side_u, side), jnp.float32),
            pltpu.VMEM(turned, jnp.bfloat16),
            pltpu.VMEM(turned, jnp.bfloat16),
            dma((owners,)), dma((n,)),
            dma((n,)), dma((owners,)),
            dma((n,)), dma((owners,)),
            dma, dma,
            dma((n,)), dma((n,)),
        ],
        compiler_params=pltpu.CompilerParams(
            collective_id=0, has_side_effects=True, vmem_limit_bytes=40 << 20
        ),
    )(field, active_rows, kern, target)


def solution(mesh):
    placed = (
        P("wa", "cand", None, "gx", None, "gy", None),
        P("gx", None),
        P("wa", None, None, None, None),
        P("wa", None, None),
    )
    return jax.shard_map(
        functools.partial(on_device, mesh.shape["gx"], mesh.shape["gy"]),
        mesh=mesh,
        in_specs=placed,
        out_specs=(P("gx", "cand", "gy", None), P("wa", "cand", None)),
        check_vma=False,
    )
```

time: 137 us -> 27.3 us (0.20)
  waiting for transfers between devices: 93.4 us -> 0 us
  Pallas kernels: 0 us -> 21.7 us
  between operations: 14.3 us -> 0.65 us
  blocking collectives: 10.6 us -> 0 us
  matrix products: 5.16 us -> 0 us
  other arithmetic: 3.59 us -> 0 us
  starting transfers between devices: 3.38 us -> 0 us
    psum x2 -> x0, waiting for transfers between devices: 90 us -> none  [the longest x1 72.8 us: on_device(): focal_real, focal_imag = lax.psum((focal_real, focal_imag), ('gx', 'gy'))]
    pallas_call x0 -> x1, Pallas kernels: none -> 21.7 us  [on_device(): pl.pallas_call(functools.partial(kernel, nx, ny), out_shape=(jax.ShapeDty...]
    all_to_all x1 -> x0, blocking collectives: 10.6 us -> none  [on_device(): lax.all_to_all(summed.astype(jnp.bfloat16), 'gx', split_axis=0, concat_ax...]
    dot_general x16 -> x0, matrix products: 5.16 us -> none  [the longest x8 3.24 us: precise(): jnp.einsum(form, first, second, precision=lax.Precision.HIGHEST, preferre...]
    all_to_all x1 -> x0, waiting for transfers between devices: 3.39 us -> none  [on_device(): lax.all_to_all(lax.all_to_all(summed.astype(jnp.bfloat16), 'gx', split_ax...]
    all_to_all x1 -> x0, starting transfers between devices: 3.3 us -> none  [on_device(): lax.all_to_all(lax.all_to_all(summed.astype(jnp.bfloat16), 'gx', split_ax...]
    unnamed x16 -> x10, local copies, waits for them, and re-layouts: 5.38 us -> 4.76 us
  transfers between devices with their start and end apart: 3 -> 0, of which waited for: 3 -> 0; matrix products, arithmetic and copies ran while one was open for 1% -> 0% of each run, Pallas kernels for 0% -> 0%
where the time goes in v1:
time: 27.3 us; the launch traced here: 27.1 us
  Pallas kernels  21.7 us (79%)
  local copies, waits for them, and re-layouts  4.76 us (17%)
  between operations  0.65 us (2%)
    pallas_call x1, Pallas kernels, on_device(): pl.pallas_call(functools.partial(kernel, nx, ny), out_shape=(jax.ShapeDty...  21.7 us
    unnamed x10, local copies, waits for them, and re-layouts  4.76 us

profile of v1, /device:TPU:0, one launch (start us, length us, event | category | flops | bytes accessed | tf_op | source)
XLA Modules:
  0.0 27.1 jit_solution(1127826200176302897)
XLA Ops:
  0.6 0.0 copy-start
  0.6 1.0 %copy-done = bf16[2,2,2,1,4,64,128]{6,5,4,3,2,1,0:T(8,128)(2,1)S(1)} copy-done((bf16[2,2,2,1,4,64,128]{6,5,4,3,2,1,0:T(8,128)(2,1)S(1)}, bf16[2,2,2,1,4,64,128]{6,5,4,3,2,1,0:T(8,128)(2,1)}, u32[]{:S(2)}) %copy-start) | copy-done | bytes 524312
  1.7 0.0 copy-start.1
  1.7 0.9 %copy-done.1 = bf16[2,2,4,64,128]{4,3,2,1,0:T(8,128)(2,1)S(1)} copy-done((bf16[2,2,4,64,128]{4,3,2,1,0:T(8,128)(2,1)S(1)}, bf16[2,2,4,64,128]{4,3,2,1,0:T(8,128)(2,1)}, u32[]{:S(2)}) %copy-start.1) | copy-done | bytes 262168
  2.6 0.0 copy-start.2
  2.6 0.8 %copy-done.2 = f32[2,64,64]{2,1,0:T(8,128)S(1)} copy-done((f32[2,64,64]{2,1,0:T(8,128)S(1)}, f32[2,64,64]{2,1,0:T(8,128)}, u32[]{:S(2)}) %copy-start.2) | copy-done | bytes 32792
  3.5 0.0 copy-start.3
  3.5 0.7 %copy-done.3 = s32[1,4]{1,0:T(1,128)S(1)} copy-done((s32[1,4]{1,0:T(1,128)S(1)}, s32[1,4]{1,0:T(1,128)}, u32[]{:S(2)}) %copy-start.3) | copy-done | bytes 40
  4.1 21.7 %shard_map.59 = (f32[1,4,64,128]{3,2,1,0:T(8,128)S(1)}, f32[2,64,64]{2,1,0:T(8,128)S(1)}) custom-call(bf16[2,2,2,1,4,64,128]{6,5,4,3,2,1,0:T(8,128)(2,1)S(1)} %copy-done, s32[1,4]{1,0:T(1,128)S(1)} %copy-done.3, bf16[2,2,4,64,128]{4,3,2,1,0:T(8,128)(2,1)S(1)} %copy-done.1, f32[2,64,64]{2,1,0:T(8,128)S(1)} %copy-done.2), custom_call_target="tpu_custom_call" | custom-call | tf_op jit(solution)/shard_map/pallas_call | solution.py:274
  25.8 0.7 %copy.8 = f32[1,4,64,128]{3,2,1,0:T(8,128)} copy(f32[1,4,64,128]{3,2,1,0:T(8,128)S(1)} %get-tuple-element.4) | data formatting | bytes 262144
  26.4 0.6 %copy.9 = f32[2,64,64]{2,1,0:T(8,128)} copy(f32[2,64,64]{2,1,0:T(8,128)S(1)} %get-tuple-element.5) | data formatting | bytes 65536
Async XLA Ops:
  0.6 1.0 %copy-start = (bf16[2,2,2,1,4,64,128]{6,5,4,3,2,1,0:T(8,128)(2,1)S(1)}, bf16[2,2,2,1,4,64,128]{6,5,4,3,2,1,0:T(8,128)(2,1)}, u32[]{:S(2)}) copy-start(bf16[2,2,2,1,4,64,128]{6,5,4,3,2,1,0:T(8,128)(2,1)} %field.1) | copy-start | bytes 1572868
  1.7 0.9 %copy-start.1 = (bf16[2,2,4,64,128]{4,3,2,1,0:T(8,128)(2,1)S(1)}, bf16[2,2,4,64,128]{4,3,2,1,0:T(8,128)(2,1)}, u32[]{:S(2)}) copy-start(bf16[2,2,4,64,128]{4,3,2,1,0:T(8,128)(2,1)} %kern.1) | copy-start | bytes 786436
  2.6 0.8 %copy-start.2 = (f32[2,64,64]{2,1,0:T(8,128)S(1)}, f32[2,64,64]{2,1,0:T(8,128)}, u32[]{:S(2)}) copy-start(f32[2,64,64]{2,1,0:T(8,128)} %target.1) | copy-start | bytes 98308
  3.5 0.7 %copy-start.3 = (s32[1,4]{1,0:T(1,128)S(1)}, s32[1,4]{1,0:T(1,128)}, u32[]{:S(2)}) copy-start(s32[1,4]{1,0:T(1,128)} %rows.1) | copy-start | bytes 52

commit v2 on v1

--- a/solution.py
+++ b/solution.py
@@ -30,8 +30,8 @@
 
 
 def kernel(
-    nx, ny, field, rows, kern, target, grad, inten,
-    plane, weights, fpart, frecv, src, ibuf, pown, ppeer, total, tsend, trecv,
+    nx, ny, field_far, rows, kern_far, target_far, grad, inten,
+    field, kern, target, field_in, kern_in, target_in, plane, weights, fpart, frecv, src, ibuf, pown, ppeer, total, tsend, trecv,
     rs_send, rs_recv, ag_send, ag_recv, in_send, in_recv, wa_send, wa_recv, tr_send, tr_recv,
 ):
     n = nx * ny
@@ -39,6 +39,18 @@
     me = gx * ny + gy
     waves, pols, _, _, tiles, side_u, side = field.shape
     fp = kern.shape[3]
+    loads = []
+    for l in range(waves):
+        loads.append(
+            (
+                pltpu.make_async_copy(kern_far.at[l], kern.at[l], kern_in.at[l]),
+                pltpu.make_async_copy(field_far.at[l], field.at[l], field_in.at[l]),
+            )
+        )
+        for copy in loads[l]:
+            copy.start()
+    goals = pltpu.make_async_copy(target_far, target, target_in)
+    goals.start()
     per_wave = fp // SHARD_ROWS
     owners = waves * per_wave
     group = side // side_u
@@ -66,6 +78,8 @@
 
     row_index = lax.broadcasted_iota(jnp.int32, (side_u, side), 0) + gy * side_u
     for l in range(waves):
+        for copy in loads[l]:
+            copy.wait()
         for j in range(tiles):
             real, imag = kern[l, 0, j], kern[l, 1, j]
             at = 2 * side * j
@@ -106,6 +120,8 @@
             @pl.when(owner != me)
             def _():
                 shard_copy(owner, me).start()
+
+    goals.wait()
 
     def source_copy(peer, slot):
         return pltpu.make_async_remote_copy(
@@ -156,6 +172,13 @@
     else:
         owned()
 
+    def swap(tile):
+        return pltpu.make_async_remote_copy(
+            src_ref=pown.at[tile], dst_ref=ppeer.at[tile],
+            send_sem=wa_send.at[tile], recv_sem=wa_recv.at[tile],
+            device_id={"wa": 1 - wa}, device_id_type=MESH,
+        )
+
     for l in range(waves):
         for k in range(per_wave):
             owner = l * per_wave + k
@@ -193,46 +216,48 @@
                 total[j] = value
             else:
                 pown[j] = (value * jnp.float32(tiles * side / fp)).astype(jnp.bfloat16)
-
-    swap = pltpu.make_async_remote_copy(
-        src_ref=pown, dst_ref=ppeer, send_sem=wa_send, recv_sem=wa_recv,
-        device_id={"wa": 1 - wa}, device_id_type=MESH,
-    )
-    swap.start()
-
-    for owner in range(owners):
-        @pl.when(owner != me)
-        def _():
-            intensity_copy(owner, owner).wait_recv()
-
-        l, first, half = owner // per_wave, owner % per_wave * SHARD_ROWS, SHARD_ROWS // 2
-        value = ibuf[owner]
-        inten[l, first : first + half, :] = value[:, : LANES // 2]
-        inten[l, first + half : first + 2 * half, :] = value[:, LANES // 2 :]
-
-    swap.wait()
+                swap(j).start()
 
     packs = tsend.shape[2] // side_u
     short = side_u // packs
-    for j in range(tiles):
-        value = pown[j].astype(jnp.float32) + ppeer[j].astype(jnp.float32)
-        total[j] = value
+
+    def turned_copy(peer, slot):
+        return pltpu.make_async_remote_copy(
+            src_ref=tsend.at[peer], dst_ref=trecv.at[slot],
+            send_sem=tr_send.at[peer], recv_sem=tr_recv.at[slot],
+            device_id=place(peer), device_id_type=MESH,
+        )
+
+    def turn(step):
+        tile = lax.rem(gx + 1 + step, tiles)
+        swap(tile).wait_recv()
+        value = pown[tile].astype(jnp.float32) + ppeer[tile].astype(jnp.float32)
+        total[tile] = value
         turned = value.T
         for k in range(ny):
             block = turned[k * side_u : (k + 1) * side_u]
             block = jnp.concatenate(
                 [block[g * short : (g + 1) * short] for g in range(packs)], axis=1
             )
-            tsend[j * ny + k] = block.astype(jnp.bfloat16)
-
-    def turned_copy(peer, slot):
-        return pltpu.make_async_remote_copy(
-            src_ref=tsend.at[peer], dst_ref=trecv.at[slot],
-            send_sem=tr_send.at[peer], recv_sem=tr_recv.at[slot],
-            device_id=place(peer), device_id_type=MESH,
-        )
-
-    each(n - 1, lambda step: turned_copy(peer_of(step), me).start())
+            peer = tile * ny + k
+            tsend[peer] = block.astype(jnp.bfloat16)
+
+            @pl.when(peer != me)
+            def _():
+                turned_copy(peer, me).start()
+
+    each(tiles, turn)
+
+    for owner in range(owners):
+        @pl.when(owner != me)
+        def _():
+            intensity_copy(owner, owner).wait_recv()
+
+        l, first, half = owner // per_wave, owner % per_wave * SHARD_ROWS, SHARD_ROWS // 2
+        value = ibuf[owner]
+        inten[l, first : first + half, :] = value[:, : LANES // 2]
+        inten[l, first + half : first + 2 * half, :] = value[:, LANES // 2 :]
+
     trecv[me] = tsend[me]
     each(n - 1, lambda step: turned_copy(me, peer_of(step)).wait_recv())
     for j in range(tiles):
@@ -243,6 +268,7 @@
         ]
         grad[0, j] = 0.5 * (total[j] + jnp.concatenate(lines, axis=0))
 
+    each(tiles, lambda tile: swap(tile).wait_send())
     for owner in range(owners):
         @pl.when(owner != me)
         def _():
@@ -270,6 +296,7 @@
     turned = (n, side_u // packs, side_u * packs)
     dma = pltpu.SemaphoreType.DMA
     vmem = pl.BlockSpec(memory_space=pltpu.VMEM)
+    far = pl.BlockSpec(memory_space=pltpu.HBM)
     width = pols * LANES
     return pl.pallas_call(
         functools.partial(kernel, nx, ny),
@@ -277,9 +304,13 @@
             jax.ShapeDtypeStruct((1, tiles, side_u, side), jnp.float32),
             jax.ShapeDtypeStruct((waves, fp, fp), jnp.float32),
         ),
-        in_specs=[vmem, pl.BlockSpec(memory_space=pltpu.SMEM), vmem, vmem],
+        in_specs=[far, pl.BlockSpec(memory_space=pltpu.SMEM), far, far],
         out_specs=(vmem, vmem),
         scratch_shapes=[
+            pltpu.VMEM(field.shape, field.dtype),
+            pltpu.VMEM(kern.shape, kern.dtype),
+            pltpu.VMEM(target.shape, target.dtype),
+            dma((waves,)), dma((waves,)), dma,
             pltpu.VMEM((waves, pols * side_u, tiles * 2 * side), jnp.bfloat16),
             pltpu.VMEM((waves, 2 * fp, tiles * 2 * side), jnp.bfloat16),
             pltpu.VMEM((owners, SHARD_ROWS, width), jnp.float32),
@@ -294,7 +325,7 @@
             dma((owners,)), dma((n,)),
             dma((n,)), dma((owners,)),
             dma((n,)), dma((owners,)),
-            dma, dma,
+            dma((tiles,)), dma((tiles,)),
             dma((n,)), dma((n,)),
         ],
         compiler_params=pltpu.CompilerParams(

time: 27.3 us -> 27.5 us (level)
  no operation moved by 1% of the time
where the time goes in v2:
time: 27.5 us; the launch traced here: 27.2 us
  Pallas kernels  21.8 us (79%)
  local copies, waits for them, and re-layouts  4.76 us (17%)
  between operations  0.65 us (2%)
    pallas_call x1, Pallas kernels, on_device(): pl.pallas_call(functools.partial(kernel, nx, ny), out_shape=(jax.ShapeDty...  21.8 us
    unnamed x10, local copies, waits for them, and re-layouts  4.76 us

profile of v2, /device:TPU:0, one launch (start us, length us, event | category | flops | bytes accessed | tf_op | source)
XLA Modules:
  0.0 27.2 jit_solution(14000741228256951339)
XLA Ops:
  0.6 0.0 copy-start
  0.6 1.0 %copy-done = bf16[2,2,2,1,4,64,128]{6,5,4,3,2,1,0:T(8,128)(2,1)S(1)} copy-done((bf16[2,2,2,1,4,64,128]{6,5,4,3,2,1,0:T(8,128)(2,1)S(1)}, bf16[2,2,2,1,4,64,128]{6,5,4,3,2,1,0:T(8,128)(2,1)}, u32[]{:S(2)}) %copy-start) | copy-done | bytes 524312
  1.7 0.0 copy-start.1
  1.7 0.9 %copy-done.1 = bf16[2,2,4,64,128]{4,3,2,1,0:T(8,128)(2,1)S(1)} copy-done((bf16[2,2,4,64,128]{4,3,2,1,0:T(8,128)(2,1)S(1)}, bf16[2,2,4,64,128]{4,3,2,1,0:T(8,128)(2,1)}, u32[]{:S(2)}) %copy-start.1) | copy-done | bytes 262168
  2.6 0.0 copy-start.2
  2.6 0.8 %copy-done.2 = f32[2,64,64]{2,1,0:T(8,128)S(1)} copy-done((f32[2,64,64]{2,1,0:T(8,128)S(1)}, f32[2,64,64]{2,1,0:T(8,128)}, u32[]{:S(2)}) %copy-start.2) | copy-done | bytes 32792
  3.5 0.0 copy-start.3
  3.5 0.7 %copy-done.3 = s32[1,4]{1,0:T(1,128)S(1)} copy-done((s32[1,4]{1,0:T(1,128)S(1)}, s32[1,4]{1,0:T(1,128)}, u32[]{:S(2)}) %copy-start.3) | copy-done | bytes 40
  4.1 21.8 %shard_map.59 = (f32[1,4,64,128]{3,2,1,0:T(8,128)S(1)}, f32[2,64,64]{2,1,0:T(8,128)S(1)}) custom-call(bf16[2,2,2,1,4,64,128]{6,5,4,3,2,1,0:T(8,128)(2,1)S(1)} %copy-done, s32[1,4]{1,0:T(1,128)S(1)} %copy-done.3, bf16[2,2,4,64,128]{4,3,2,1,0:T(8,128)(2,1)S(1)} %copy-done.1, f32[2,64,64]{2,1,0:T(8,128)S(1)} %copy-done.2), custom_call_target="tpu_custom_call" | custom-call | tf_op jit(solution)/shard_map/pallas_call | solution.py:301
  25.9 0.7 %copy.8 = f32[1,4,64,128]{3,2,1,0:T(8,128)} copy(f32[1,4,64,128]{3,2,1,0:T(8,128)S(1)} %get-tuple-element.4) | data formatting | bytes 262144
  26.6 0.6 %copy.9 = f32[2,64,64]{2,1,0:T(8,128)} copy(f32[2,64,64]{2,1,0:T(8,128)S(1)} %get-tuple-element.5) | data formatting | bytes 65536
Async XLA Ops:
  0.6 1.0 %copy-start = (bf16[2,2,2,1,4,64,128]{6,5,4,3,2,1,0:T(8,128)(2,1)S(1)}, bf16[2,2,2,1,4,64,128]{6,5,4,3,2,1,0:T(8,128)(2,1)}, u32[]{:S(2)}) copy-start(bf16[2,2,2,1,4,64,128]{6,5,4,3,2,1,0:T(8,128)(2,1)} %field_far.1) | copy-start | bytes 1572868
  1.7 0.9 %copy-start.1 = (bf16[2,2,4,64,128]{4,3,2,1,0:T(8,128)(2,1)S(1)}, bf16[2,2,4,64,128]{4,3,2,1,0:T(8,128)(2,1)}, u32[]{:S(2)}) copy-start(bf16[2,2,4,64,128]{4,3,2,1,0:T(8,128)(2,1)} %kern_far.1) | copy-start | bytes 786436
  2.6 0.8 %copy-start.2 = (f32[2,64,64]{2,1,0:T(8,128)S(1)}, f32[2,64,64]{2,1,0:T(8,128)}, u32[]{:S(2)}) copy-start(f32[2,64,64]{2,1,0:T(8,128)} %target_far.1) | copy-start | bytes 98308
  3.5 0.7 %copy-start.3 = (s32[1,4]{1,0:T(1,128)S(1)}, s32[1,4]{1,0:T(1,128)}, u32[]{:S(2)}) copy-start(s32[1,4]{1,0:T(1,128)} %rows.1) | copy-start | bytes 52

commit v3 on v2

--- a/solution.py
+++ b/solution.py
@@ -329,7 +329,7 @@
             dma((n,)), dma((n,)),
         ],
         compiler_params=pltpu.CompilerParams(
-            collective_id=0, has_side_effects=True, vmem_limit_bytes=40 << 20
+            collective_id=0, has_side_effects=True, vmem_limit_bytes=64 << 20
         ),
     )(field, active_rows, kern, target)
 

time: 27.5 us -> 25.6 us (0.931)
  local copies, waits for them, and re-layouts: 4.76 us -> 2.23 us
  Pallas kernels: 21.8 us -> 22.5 us
    unnamed x10 -> x4, local copies, waits for them, and re-layouts: 4.76 us -> 2.23 us
    pallas_call x1, Pallas kernels: 21.8 us -> 22.5 us  [on_device(): pl.pallas_call(functools.partial(kernel, nx, ny), out_shape=(jax.ShapeDty...]
where the time goes in v3:
time: 25.6 us; the launch traced here: 25.4 us
  Pallas kernels  22.5 us (88%)
  local copies, waits for them, and re-layouts  2.23 us (9%)
  between operations  0.65 us (3%)
    pallas_call x1, Pallas kernels, on_device(): pl.pallas_call(functools.partial(kernel, nx, ny), out_shape=(jax.ShapeDty...  22.5 us
    unnamed x4, local copies, waits for them, and re-layouts  2.23 us

profile of v3, /device:TPU:0, one launch (start us, length us, event | category | flops | bytes accessed | tf_op | source)
XLA Modules:
  0.0 25.4 jit_solution(13281459831385832155)
XLA Ops:
  0.6 22.5 %shard_map.59 = (f32[1,4,64,128]{3,2,1,0:T(8,128)}, f32[2,64,64]{2,1,0:T(8,128)}) custom-call(bf16[2,2,2,1,4,64,128]{6,5,4,3,2,1,0:T(8,128)(2,1)} %field_far.1, s32[1,4]{1,0:T(1,128)} %rows.1, bf16[2,2,4,64,128]{4,3,2,1,0:T(8,128)(2,1)} %kern_far.1, f32[2,64,64]{2,1,0:T(8,128)} %target_far.1), custom_call_target="tpu_custom_call" | custom-call | tf_op jit(solution)/shard_map/pallas_call | solution.py:301
  23.2 0.0 copy-start
  23.2 1.6 %copy.8 = f32[1,4,64,128]{3,2,1,0:T(8,128)} copy(f32[1,4,64,128]{3,2,1,0:T(8,128)} %get-tuple-element.4) | data formatting | bytes 262144
  24.8 0.0 copy-done
  24.8 0.6 %copy.9 = f32[2,64,64]{2,1,0:T(8,128)} copy(f32[2,64,64]{2,1,0:T(8,128)S(1)} %copy-done) | data formatting | bytes 65536
Async XLA Ops:
  23.2 1.6 %copy-start = (f32[2,64,64]{2,1,0:T(8,128)S(1)}, f32[2,64,64]{2,1,0:T(8,128)}, u32[]{:S(2)}) copy-start(f32[2,64,64]{2,1,0:T(8,128)} %get-tuple-element.5) | copy-start | bytes 98308

commit v4 on v3

--- a/solution.py
+++ b/solution.py
@@ -111,7 +111,9 @@
             own, low, preferred_element_type=jnp.float32
         )
         for k in range(per_wave):
-            fpart[l * per_wave + k] = focal[k * SHARD_ROWS : (k + 1) * SHARD_ROWS]
+            fpart[l * per_wave + k] = focal[k * SHARD_ROWS : (k + 1) * SHARD_ROWS].astype(
+                jnp.bfloat16
+            )
         if l == 0:
             pl.semaphore_wait(barrier, n)
         for k in range(per_wave):
@@ -145,12 +147,13 @@
 
         each(n - 1, arrive)
         if n <= 16:
-            focal = frecv[0]
+            focal = frecv[0].astype(jnp.float32)
             for slot in range(1, n):
-                focal = focal + frecv[slot]
+                focal = focal + frecv[slot].astype(jnp.float32)
         else:
             focal = lax.fori_loop(
-                1, n, lambda slot, value: value + frecv[slot], frecv[0]
+                1, n, lambda slot, value: value + frecv[slot].astype(jnp.float32),
+                frecv[0].astype(jnp.float32),
             )
         square = focal * focal
         bright = square[:, :LANES]
@@ -313,8 +316,8 @@
             dma((waves,)), dma((waves,)), dma,
             pltpu.VMEM((waves, pols * side_u, tiles * 2 * side), jnp.bfloat16),
             pltpu.VMEM((waves, 2 * fp, tiles * 2 * side), jnp.bfloat16),
-            pltpu.VMEM((owners, SHARD_ROWS, width), jnp.float32),
-            pltpu.VMEM((n, SHARD_ROWS, width), jnp.float32),
+            pltpu.VMEM((owners, SHARD_ROWS, width), jnp.bfloat16),
+            pltpu.VMEM((n, SHARD_ROWS, width), jnp.bfloat16),
             pltpu.VMEM((owners, SHARD_ROWS, width), jnp.bfloat16),
             pltpu.VMEM((owners, SHARD_ROWS // 2, LANES), jnp.float32),
             pltpu.VMEM((tiles, side_u, side), jnp.bfloat16),

time: 25.6 us -> 24.6 us (0.961)
  Pallas kernels: 22.5 us -> 21.5 us
    pallas_call x1, Pallas kernels: 22.5 us -> 21.5 us  [on_device(): pl.pallas_call(functools.partial(kernel, nx, ny), out_shape=(jax.ShapeDty...]
where the time goes in v4:
time: 24.6 us; the launch traced here: 24.4 us
  Pallas kernels  21.5 us (87%)
  local copies, waits for them, and re-layouts  2.23 us (9%)
  between operations  0.65 us (3%)
    pallas_call x1, Pallas kernels, on_device(): pl.pallas_call(functools.partial(kernel, nx, ny), out_shape=(jax.ShapeDty...  21.5 us
    unnamed x4, local copies, waits for them, and re-layouts  2.23 us

profile of v4, /device:TPU:0, one launch (start us, length us, event | category | flops | bytes accessed | tf_op | source)
XLA Modules:
  0.0 24.4 jit_solution(12283922640901593368)
XLA Ops:
  0.6 21.5 %shard_map.59 = (f32[1,4,64,128]{3,2,1,0:T(8,128)}, f32[2,64,64]{2,1,0:T(8,128)}) custom-call(bf16[2,2,2,1,4,64,128]{6,5,4,3,2,1,0:T(8,128)(2,1)} %field_far.1, s32[1,4]{1,0:T(1,128)} %rows.1, bf16[2,2,4,64,128]{4,3,2,1,0:T(8,128)(2,1)} %kern_far.1, f32[2,64,64]{2,1,0:T(8,128)} %target_far.1), custom_call_target="tpu_custom_call" | custom-call | tf_op jit(solution)/shard_map/pallas_call | solution.py:304
  22.2 0.0 copy-start
  22.2 1.6 %copy.8 = f32[1,4,64,128]{3,2,1,0:T(8,128)} copy(f32[1,4,64,128]{3,2,1,0:T(8,128)} %get-tuple-element.4) | data formatting | bytes 262144
  23.8 0.0 copy-done
  23.8 0.6 %copy.9 = f32[2,64,64]{2,1,0:T(8,128)} copy(f32[2,64,64]{2,1,0:T(8,128)S(1)} %copy-done) | data formatting | bytes 65536
Async XLA Ops:
  22.2 1.6 %copy-start = (f32[2,64,64]{2,1,0:T(8,128)S(1)}, f32[2,64,64]{2,1,0:T(8,128)}, u32[]{:S(2)}) copy-start(f32[2,64,64]{2,1,0:T(8,128)} %get-tuple-element.5) | copy-start | bytes 98308

commit v5 on v4

--- a/solution.py
+++ b/solution.py
@@ -288,6 +288,20 @@
     each(n - 1, lambda step: turned_copy(peer_of(step), me).wait_send())
 
 
+def deliver(grad, inten, grad_out, inten_out, grad_sems, inten_sems):
+    copies = [
+        pltpu.make_async_copy(grad.at[0, j], grad_out.at[0, j], grad_sems.at[j])
+        for j in range(grad.shape[1])
+    ] + [
+        pltpu.make_async_copy(inten.at[l], inten_out.at[l], inten_sems.at[l])
+        for l in range(inten.shape[0])
+    ]
+    for copy in copies:
+        copy.start()
+    for copy in copies:
+        copy.wait()
+
+
 def on_device(nx, ny, field, active_rows, kern, target):
     waves, pols, _, _, tiles, side_u, side = field.shape
     fp = kern.shape[3]
@@ -301,12 +315,13 @@
     vmem = pl.BlockSpec(memory_space=pltpu.VMEM)
     far = pl.BlockSpec(memory_space=pltpu.HBM)
     width = pols * LANES
-    return pl.pallas_call(
+    results = (
+        jax.ShapeDtypeStruct((1, tiles, side_u, side), jnp.float32),
+        jax.ShapeDtypeStruct((waves, fp, fp), jnp.float32),
+    )
+    grad, inten = pl.pallas_call(
         functools.partial(kernel, nx, ny),
-        out_shape=(
-            jax.ShapeDtypeStruct((1, tiles, side_u, side), jnp.float32),
-            jax.ShapeDtypeStruct((waves, fp, fp), jnp.float32),
-        ),
+        out_shape=results,
         in_specs=[far, pl.BlockSpec(memory_space=pltpu.SMEM), far, far],
         out_specs=(vmem, vmem),
         scratch_shapes=[
@@ -335,6 +350,14 @@
             collective_id=0, has_side_effects=True, vmem_limit_bytes=64 << 20
         ),
     )(field, active_rows, kern, target)
+    return pl.pallas_call(
+        deliver,
+        out_shape=results,
+        in_specs=[far, far],
+        out_specs=(far, far),
+        scratch_shapes=[dma((tiles,)), dma((waves,))],
+        compiler_params=pltpu.CompilerParams(vmem_limit_bytes=64 << 20),
+    )(grad, inten)
 
 
 def solution(mesh):

time: 24.6 us -> 29.5 us (1.20)
  Pallas kernels: 21.5 us -> 28.7 us
  local copies, waits for them, and re-layouts: 2.23 us -> 0 us
    pallas_call x1 -> x2, Pallas kernels: 21.5 us -> 28.7 us  [the longest x1 21.6 us: on_device(): pl.pallas_call(functools.partial(kernel, nx, ny), out_shape=results, in_s...]
    unnamed x4 -> x0, local copies, waits for them, and re-layouts: 2.23 us -> none
where the time goes in v5:
time: 29.5 us; the launch traced here: 29.3 us
  Pallas kernels  28.7 us (97%)
  between operations  0.64 us (2%)
    pallas_call x1, Pallas kernels, on_device(): pl.pallas_call(functools.partial(kernel, nx, ny), out_shape=results, in_s...  21.6 us
    pallas_call x1, Pallas kernels, on_device(): pl.pallas_call(deliver, out_shape=results, in_specs=[far, far], out_specs...  7.11 us

profile of v5, /device:TPU:0, one launch (start us, length us, event | category | flops | bytes accessed | tf_op | source)
XLA Modules:
  0.0 29.3 jit_solution(924796243018699573)
XLA Ops:
  0.6 21.6 %shard_map.59 = (f32[1,4,64,128]{3,2,1,0:T(8,128)}, f32[2,64,64]{2,1,0:T(8,128)}) custom-call(bf16[2,2,2,1,4,64,128]{6,5,4,3,2,1,0:T(8,128)(2,1)} %field_far.1, s32[1,4]{1,0:T(1,128)} %rows.1, bf16[2,2,4,64,128]{4,3,2,1,0:T(8,128)(2,1)} %kern_far.1, f32[2,64,64]{2,1,0:T(8,128)} %target_far.1), custom_call_target="tpu_custom_call" | custom-call | tf_op jit(solution)/shard_map/pallas_call | solution.py:322
  22.2 7.1 %shard_map.60 = (f32[1,4,64,128]{3,2,1,0:T(8,128)}, f32[2,64,64]{2,1,0:T(8,128)}) custom-call(f32[1,4,64,128]{3,2,1,0:T(8,128)} %get-tuple-element.4.grad, f32[2,64,64]{2,1,0:T(8,128)} %get-tuple-element.5.inten), custom_call_target="tpu_custom_call" | custom-call | tf_op jit(solution)/shard_map/pallas_call | solution.py:353

commit v6 on v4

--- a/solution.py
+++ b/solution.py
@@ -30,8 +30,8 @@
 
 
 def kernel(
-    nx, ny, field_far, rows, kern_far, target_far, grad, inten,
-    field, kern, target, field_in, kern_in, target_in, plane, weights, fpart, frecv, src, ibuf, pown, ppeer, total, tsend, trecv,
+    nx, ny, field_far, rows, kern_far, target_far, grad_far, inten_far,
+    grad, inten, grad_out, inten_out, field, kern, target, field_in, kern_in, target_in, plane, weights, fpart, frecv, src, ibuf, pown, ppeer, total, tsend, trecv,
     rs_send, rs_recv, ag_send, ag_recv, in_send, in_recv, wa_send, wa_recv, tr_send, tr_recv,
 ):
     n = nx * ny
@@ -261,15 +261,32 @@
         inten[l, first : first + half, :] = value[:, : LANES // 2]
         inten[l, first + half : first + 2 * half, :] = value[:, LANES // 2 :]
 
+    inten_done = pltpu.make_async_copy(inten, inten_far, inten_out)
+    inten_done.start()
+
+    def grad_done(tile):
+        return pltpu.make_async_copy(grad.at[tile], grad_far.at[0, tile], grad_out.at[tile])
+
     trecv[me] = tsend[me]
-    each(n - 1, lambda step: turned_copy(me, peer_of(step)).wait_recv())
-    for j in range(tiles):
-        blocks = [trecv[j * ny + k].astype(jnp.float32) for k in range(ny)]
+
+    def finish(step):
+        tile = lax.rem(gx + step, tiles)
+        for k in range(ny):
+            peer = tile * ny + k
+
+            @pl.when(peer != me)
+            def _():
+                turned_copy(me, peer).wait_recv()
+
+        blocks = [trecv[tile * ny + k].astype(jnp.float32) for k in range(ny)]
         lines = [
             jnp.concatenate([block[:, g * side_u : (g + 1) * side_u] for block in blocks], axis=1)
             for g in range(packs)
         ]
-        grad[0, j] = 0.5 * (total[j] + jnp.concatenate(lines, axis=0))
+        grad[tile] = 0.5 * (total[tile] + jnp.concatenate(lines, axis=0))
+        grad_done(tile).start()
+
+    each(tiles, finish)
 
     each(tiles, lambda tile: swap(tile).wait_send())
     for owner in range(owners):
@@ -286,6 +303,8 @@
     else:
         drain_owned()
     each(n - 1, lambda step: turned_copy(peer_of(step), me).wait_send())
+    inten_done.wait()
+    each(tiles, lambda tile: grad_done(tile).wait())
 
 
 def on_device(nx, ny, field, active_rows, kern, target):
@@ -298,7 +317,6 @@
         packs = 1
     turned = (n, side_u // packs, side_u * packs)
     dma = pltpu.SemaphoreType.DMA
-    vmem = pl.BlockSpec(memory_space=pltpu.VMEM)
     far = pl.BlockSpec(memory_space=pltpu.HBM)
     width = pols * LANES
     return pl.pallas_call(
@@ -308,8 +326,11 @@
             jax.ShapeDtypeStruct((waves, fp, fp), jnp.float32),
         ),
         in_specs=[far, pl.BlockSpec(memory_space=pltpu.SMEM), far, far],
-        out_specs=(vmem, vmem),
+        out_specs=(far, far),
         scratch_shapes=[
+            pltpu.VMEM((tiles, side_u, side), jnp.float32),
+            pltpu.VMEM((waves, fp, fp), jnp.float32),
+            dma((tiles,)), dma,
             pltpu.VMEM(field.shape, field.dtype),
             pltpu.VMEM(kern.shape, kern.dtype),
             pltpu.VMEM(target.shape, target.dtype),

time: 24.6 us -> 24.6 us (level)
  no operation moved by 1% of the time
where the time goes in v6:
time: 24.6 us; the launch traced here: 24.4 us
  Pallas kernels  21.5 us (87%)
  local copies, waits for them, and re-layouts  2.23 us (9%)
  between operations  0.65 us (3%)
    pallas_call x1, Pallas kernels, on_device(): pl.pallas_call(functools.partial(kernel, nx, ny), out_shape=(jax.ShapeDty...  21.5 us
    unnamed x4, local copies, waits for them, and re-layouts  2.23 us

profile of v6, /device:TPU:0, one launch (start us, length us, event | category | flops | bytes accessed | tf_op | source)
XLA Modules:
  0.0 24.4 jit_solution(16124756682954340266)
XLA Ops:
  0.6 21.5 %shard_map.59 = (f32[1,4,64,128]{3,2,1,0:T(8,128)}, f32[2,64,64]{2,1,0:T(8,128)}) custom-call(bf16[2,2,2,1,4,64,128]{6,5,4,3,2,1,0:T(8,128)(2,1)} %field_far.1, s32[1,4]{1,0:T(1,128)} %rows.1, bf16[2,2,4,64,128]{4,3,2,1,0:T(8,128)(2,1)} %kern_far.1, f32[2,64,64]{2,1,0:T(8,128)} %target_far.1), custom_call_target="tpu_custom_call" | custom-call | tf_op jit(solution)/shard_map/pallas_call | solution.py:322
  22.2 0.0 copy-start
  22.2 1.6 %copy.8 = f32[1,4,64,128]{3,2,1,0:T(8,128)} copy(f32[1,4,64,128]{3,2,1,0:T(8,128)} %get-tuple-element.4) | data formatting | bytes 262144
  23.8 0.0 copy-done
  23.8 0.6 %copy.9 = f32[2,64,64]{2,1,0:T(8,128)} copy(f32[2,64,64]{2,1,0:T(8,128)S(1)} %copy-done) | data formatting | bytes 65536
Async XLA Ops:
  22.2 1.6 %copy-start = (f32[2,64,64]{2,1,0:T(8,128)S(1)}, f32[2,64,64]{2,1,0:T(8,128)}, u32[]{:S(2)}) copy-start(f32[2,64,64]{2,1,0:T(8,128)} %get-tuple-element.5) | copy-start | bytes 98308

commit v7 on v4

--- a/solution.py
+++ b/solution.py
@@ -332,7 +332,7 @@
             dma((n,)), dma((n,)),
         ],
         compiler_params=pltpu.CompilerParams(
-            collective_id=0, has_side_effects=True, vmem_limit_bytes=64 << 20
+            collective_id=0, has_side_effects=True, vmem_limit_bytes=54848 << 10
         ),
     )(field, active_rows, kern, target)
 

time: 24.6 us -> 24.4 us (level)
  Pallas kernels: 21.5 us -> 20.8 us
  local copies, waits for them, and re-layouts: 2.23 us -> 2.77 us
    pallas_call x1, Pallas kernels: 21.5 us -> 20.8 us  [on_device(): pl.pallas_call(functools.partial(kernel, nx, ny), out_shape=(jax.ShapeDty...]
    unnamed x4 -> x6, local copies, waits for them, and re-layouts: 2.23 us -> 2.77 us
where the time goes in v7:
time: 24.4 us; the launch traced here: 24.2 us
  Pallas kernels  20.8 us (85%)
  local copies, waits for them, and re-layouts  2.77 us (11%)
  between operations  0.65 us (3%)
    pallas_call x1, Pallas kernels, on_device(): pl.pallas_call(functools.partial(kernel, nx, ny), out_shape=(jax.ShapeDty...  20.8 us
    unnamed x6, local copies, waits for them, and re-layouts  2.77 us

profile of v7, /device:TPU:0, one launch (start us, length us, event | category | flops | bytes accessed | tf_op | source)
XLA Modules:
  0.0 24.2 jit_solution(2212487868749619676)
XLA Ops:
  0.6 0.0 copy-start
  0.6 0.8 %copy-done = f32[2,64,64]{2,1,0:T(8,128)S(1)} copy-done((f32[2,64,64]{2,1,0:T(8,128)S(1)}, f32[2,64,64]{2,1,0:T(8,128)}, u32[]{:S(2)}) %copy-start) | copy-done | bytes 32792
  1.5 0.0 copy-start.1
  1.5 0.7 %copy-done.1 = s32[1,4]{1,0:T(1,128)S(1)} copy-done((s32[1,4]{1,0:T(1,128)S(1)}, s32[1,4]{1,0:T(1,128)}, u32[]{:S(2)}) %copy-start.1) | copy-done | bytes 40
  2.1 20.8 %shard_map.59 = (f32[1,4,64,128]{3,2,1,0:T(8,128)S(1)}, f32[2,64,64]{2,1,0:T(8,128)S(1)}) custom-call(bf16[2,2,2,1,4,64,128]{6,5,4,3,2,1,0:T(8,128)(2,1)} %field_far.1, s32[1,4]{1,0:T(1,128)S(1)} %copy-done.1, bf16[2,2,4,64,128]{4,3,2,1,0:T(8,128)(2,1)} %kern_far.1, f32[2,64,64]{2,1,0:T(8,128)S(1)} %copy-done), custom_call_target="tpu_custom_call" | custom-call | tf_op jit(solution)/shard_map/pallas_call | solution.py:304
  23.0 0.7 %copy.8 = f32[1,4,64,128]{3,2,1,0:T(8,128)} copy(f32[1,4,64,128]{3,2,1,0:T(8,128)S(1)} %get-tuple-element.4) | data formatting | bytes 262144
  23.6 0.6 %copy.9 = f32[2,64,64]{2,1,0:T(8,128)} copy(f32[2,64,64]{2,1,0:T(8,128)S(1)} %get-tuple-element.5) | data formatting | bytes 65536
Async XLA Ops:
  0.6 0.8 %copy-start = (f32[2,64,64]{2,1,0:T(8,128)S(1)}, f32[2,64,64]{2,1,0:T(8,128)}, u32[]{:S(2)}) copy-start(f32[2,64,64]{2,1,0:T(8,128)} %target_far.1) | copy-start | bytes 98308
  1.5 0.7 %copy-start.1 = (s32[1,4]{1,0:T(1,128)S(1)}, s32[1,4]{1,0:T(1,128)}, u32[]{:S(2)}) copy-start(s32[1,4]{1,0:T(1,128)} %rows.1) | copy-start | bytes 52
